TPU v7x, 256 devices: a whole 4x4x8 slice. The times are simulated.
256 devices in a mesh: row: 32 (over z, x_lo, core), col: 8 (over y, x_hi).
Axes of the slice: x: 4 (x_hi: 2, x_lo: 2; x = x_hi * 2 + x_lo), y: 4, z: 8, core: 2. Of those that a mesh axis runs over, the one named last changes fastest.
Arguments:
- activations: bfloat16 [768, 28672], P('row', 'col'), may hold values from -6 to 6
- out_grads: bfloat16 [768, 8192], P('col', 'row'), may hold values from -0.3046875 to 0.3046875
- in_basis: bfloat16 [28672, 28672], P('col', 'row'), may hold values from -0.03125 to 0.03125
- out_basis: bfloat16 [8192, 8192], P('row', 'col'), may hold values from -0.0625 to 0.0625
Outputs:
- correction: float32 [28672, 8192], P('row', 'col')
All inputs are finite; a program needn't handle non-finite values.
Results may differ from a plain program's by a relative error of at most 0.0042.
Values may be sent and summed in bfloat16 or wider, within the bound.
A program may use at most 64 MiB of HBM per device.

v0:
```python
import jax
import jax.numpy as jnp
from jax import lax
from jax.sharding import PartitionSpec as P

SEQ_LEN = 384
SEQS = 2


def on_device(activations, out_grads, in_basis, out_basis):
    act_partial = jnp.dot(
        lax.all_gather(activations, "row", axis=0, tiled=True),
        in_basis,
        preferred_element_type=jnp.float32,
    )
    act_rotated = lax.psum(act_partial, "col").astype(jnp.bfloat16)
    grad_partial = jnp.dot(
        lax.all_gather(out_grads, "col", axis=0, tiled=True),
        out_basis,
        preferred_element_type=jnp.float32,
    )
    grad_rotated = lax.psum(grad_partial, "row").astype(jnp.bfloat16)
    accumulated = jnp.zeros((act_rotated.shape[1], grad_rotated.shape[1]), jnp.float32)
    for number in range(SEQS):
        act_seq = act_rotated[number * SEQ_LEN : (number + 1) * SEQ_LEN]
        grad_seq = grad_rotated[number * SEQ_LEN : (number + 1) * SEQ_LEN]
        seq_tile = lax.dot_general(
            act_seq, grad_seq, (((0,), (0,)), ((), ())), preferred_element_type=jnp.float32
        )
        accumulated = accumulated + seq_tile * seq_tile
    return accumulated / jnp.float32(SEQS)


def solution(mesh):
    placed = (P("row", "col"), P("col", "row"), P("col", "row"), P("row", "col"))
    return jax.shard_map(
        on_device, mesh=mesh, in_specs=placed, out_specs=P("row", "col"), check_vma=False
    )
```

profile of v0, /device:TPU:98, one launch (start us, length us, event | category | flops | bytes accessed | tf_op | source)
XLA Modules:
  0.0 318.3 jit_solution(5931963016922075794)
XLA Ops:
  6.5 0.0 copy-start
  6.5 0.0 all-gather.2.cloned.1.call-start
  6.5 0.7 all-gather.2.cloned.1.call-update
  7.3 35.9 %all_gather.7 = bf16[768,256]{1,0:T(8,128)(2,1)S(1)} all-gather(bf16[96,256]{1,0:T(8,128)(2,1)} %param.5), channel_id=1, replica_groups=mesh['row'=32,'col'=8] {'col'}, dimensions={0}, use_global_device_ids=true | all-gather | bytes 442368 | tf_op jit(solution)/shard_map/all_gather | solution.py:18
  43.2 0.0 copy-done
  43.2 2.2 fusion.6
  45.5 131.5 %all-reduce.3 = bf16[768,1024]{1,0:T(8,128)(2,1)S(1)} all-reduce(f32[768,1024]{1,0:T(8,128)} %fusion.6), channel_id=1, replica_groups=mesh['row'=32,'col'=8] {'row'}, use_global_device_ids=true, to_apply=%region_1.0 | all-reduce | flops 786432 | bytes 4718592 | tf_op jit(solution)/shard_map/psum | solution.py:22
  176.9 0.0 all-gather.2.cloned.1.call-done
  177.0 10.8 %fusion.5 = f32[768,896]{1,0:T(8,128)} fusion(bf16[768,3584]{1,0:T(8,128)(2,1)} %all-gather.2.cloned.1.call-done, bf16[3584,896]{1,0:T(8,128)(2,1)} %param.6), kind=kOutput, calls=%fused_computation.6 | convolution fusion | flops 4932501504 | bytes 14680064 | tf_op jit(solution)/shard_map/dot_general | solution.py:11
  187.7 119.4 %all-reduce.2 = bf16[768,896]{1,0:T(8,128)(2,1)S(1)} all-reduce(f32[768,896]{1,0:T(8,128)} %fusion.5), channel_id=1, replica_groups=mesh['row'=32,'col'=8] {'col'}, use_global_device_ids=true, to_apply=%region_0.0 | all-reduce | flops 688128 | bytes 4128768 | tf_op jit(solution)/shard_map/psum | solution.py:16
  307.2 1.1 fusion.1
  308.3 3.1 add_multiply_fusion
Async XLA Ops:
  6.5 36.7 %copy-start = (bf16[256,1024]{1,0:T(8,128)(2,1)S(1)}, bf16[256,1024]{1,0:T(8,128)(2,1)}, u32[]{:S(2)}) copy-start(bf16[256,1024]{1,0:T(8,128)(2,1)} %param.7) | copy-start | bytes 1572868
  6.5 170.4 %all-gather.2.cloned.1.call-start = ((), (), s32[]{:S(2)}) async-start(), calls=%async_computation | async-start | bytes 5677056 | tf_op jit(solution)/shard_map/all_gather | solution.py:12
Sparse Core Ops, SparseCore 0:
  9.2 71.0 all-gather.1
where the time goes:
time: 318 us
  blocking collectives  287 us (90%)
  matrix products  17.3 us (5%)
  between operations  13.4 us (4%)
    psum x1, blocking collectives, on_device(): grad_rotated = lax.psum(grad_partial, 'row').astype(jnp.bfloat16)  131 us
    psum x1, blocking collectives, on_device(): act_rotated = lax.psum(act_partial, 'col').astype(jnp.bfloat16)  119 us
    all_gather x1, blocking collectives, on_device(): lax.all_gather(out_grads, 'col', axis=0, tiled=True)  35.9 us
    dot_general x1, matrix products, on_device(): jnp.dot(lax.all_gather(activations, 'row', axis=0, tiled=True), in_basis,...  10.8 us
  transfers between devices with their start and end apart: 1, of which 0 were waited for; matrix products, arithmetic and copies ran while one was open for 1% of the time, Pallas kernels for 0%

commit v1 on v0

v1 whole, which is shorter than its diff:
```python
import functools

import jax
import jax.numpy as jnp
from jax import lax
from jax.experimental import pallas as pl
from jax.experimental.pallas import tpu as pltpu
from jax.sharding import PartitionSpec as P

MESH = pl.DeviceIdType.MESH
F32 = jnp.float32
BF16 = jnp.bfloat16
NZ, NY = 8, 4
COPIES = 180
VMEM_LIMIT = 58 * 2**20


def ring(value, size):
    return lax.rem(value + size, size)


def exchange(
    act_ref, grad_ref, in_basis, out_basis, act_out, grad_out,
    basis, obasis, pair, acts, part, send_y, recv_y, own_y, half_x, recv_x, done_x, rot_raw, rot,
    grads, gsend, grecv, gown, gx_send, gx_recv, gsum, ring_send, ring_recv, grot,
    send_sem, recv_sem, local_sem,
):
    row, col = lax.axis_index("row"), lax.axis_index("col")
    z, xl, core = row // 4, lax.rem(row // 2, 2), lax.rem(row, 2)
    y, xh = col // 2, lax.rem(col, 2)

    def at(z=z, xl=xl, core=core, y=y, xh=xh):
        return (z * 4 + xl * 2 + core, y * 2 + xh)

    sibling, beside, across = at(core=1 - core), at(xl=1 - xl), at(xh=1 - xh)
    up = (at(z=ring(z + 1, NZ)), at(z=ring(z - 1, NZ)))
    around = [at(y=ring(y + rel, NY)) for rel in (1, 2, 3)]
    ids, sent = {}, []

    def copy(key, src, dst, device):
        number = ids.setdefault(key, len(ids))
        return pltpu.make_async_remote_copy(
            src_ref=src, dst_ref=dst, send_sem=send_sem.at[number], recv_sem=recv_sem.at[number],
            device_id=device, device_id_type=MESH,
        )

    def send(key, src, dst, device):
        one = copy(key, src, dst, device)
        one.start()
        sent.append(one)

    def arrive(key, dst):
        copy(key, dst, dst, sibling).wait_recv()

    load_basis = pltpu.make_async_copy(in_basis, basis, local_sem.at[0])
    load_obasis = pltpu.make_async_copy(out_basis, obasis, local_sem.at[1])
    load_obasis.start()
    load_basis.start()

    barrier = pltpu.get_barrier_semaphore()
    near = [sibling, beside, across, *up, *around]
    for device in near:
        pl.semaphore_signal(barrier, inc=1, device_id=device, device_id_type=MESH)
    half = act_ref.shape[1] // 2
    quarter = half // 2
    mine = act_ref[...].astype(F32)
    for number in range(2):
        pair[2 + number] = mine[:, number * half : (number + 1) * half]
    pair[core] = pair[2 + core]
    grads[col] = grad_ref[...]
    pl.semaphore_wait(barrier, len(near))

    send("pair", pair.at[3 - core], pair.at[core], sibling)

    send(("g1", 0), grads.at[col], grads.at[col], across)
    for rel in (1, 2, 3):
        send(("g1", rel, 0), grads.at[col], grads.at[col], around[rel - 1])

    arrive("pair", pair.at[1 - core])

    def act_slot(zz, q, part_no, side=0):
        kk = core if side == 0 else 1 - core
        return acts.at[kk, part_no, zz, xl if q == 0 else 1 - xl]

    def grad_slot(zz, q, part_no, side=0):
        kk = core if side == 0 else 1 - core
        return grot.at[2 * kk + (xl if q == 0 else 1 - xl), zz, pl.ds(96 * part_no, 96)]

    def place(zoff):
        return ring(z + zoff, NZ)

    def gather_put(name, slot, q, part_no):
        ref = slot(z, q, part_no)
        for way in (0, 1):
            send((name, way, 1, q, part_no), ref, ref, up[way])
        if q == 0:
            send((name, "x", part_no), ref, ref, beside)
        send((name, "sib", 0, q, part_no), ref, ref, sibling)

    def gather_beside(name, slot, part_no):
        arrive((name, "x", part_no), slot(z, 1, part_no))
        gather_put(name, slot, 1, part_no)

    def gather_step(name, slot, step, way, q, part_no):
        if step == 4 and part_no != way:
            return
        zoff = -step if way == 0 else step
        ref = slot(place(zoff), q, part_no)
        arrive((name, way, step, q, part_no), ref)
        if step < 3 or (step == 3 and part_no == way):
            send((name, way, step + 1, q, part_no), ref, ref, up[way])
        send((name, "sib", 4 if step == 4 else zoff, q, part_no), ref, ref, sibling)

    def gather_steps(name, slot, step):
        for q in (0, 1):
            for part_no in (0, 1):
                for way in (0, 1):
                    gather_step(name, slot, step, way, q, part_no)

    def gather_sibling(name, slot, zoff):
        for q in (0, 1):
            for part_no in (0, 1):
                arrive((name, "sib", zoff, q, part_no), slot(place(zoff), q, part_no, 1))

    block = pair[0:2].reshape(48, half).astype(BF16)
    for part_no in (0, 1):
        acts[core, part_no, z, xl] = block[:, part_no * quarter : (part_no + 1) * quarter]
    for part_no in (0, 1):
        gather_put("a", act_slot, 0, part_no)

    other = y * 2 + 1 - xh
    arrive(("g1", 0), grads.at[other])
    for rel in (1, 2, 3):
        send(("g1", rel, 1), grads.at[other], grads.at[other], around[rel - 1])
    for part_no in (0, 1):
        gather_beside("a", act_slot, part_no)

    for rel in (1, 2, 3):
        came = ring(y - rel, NY) * 2
        arrive(("g1", rel, 0), grads.at[came + xh])
        arrive(("g1", rel, 1), grads.at[came + 1 - xh])

    load_obasis.wait()

    def partial(seq, ref):
        got = jnp.dot(grads[pl.ds(4 * seq, 4)].reshape(384, 256), obasis[...], preferred_element_type=F32)
        for side in range(2):
            for zc in range(NZ):
                ref[side, zc] = got[192 * side : 192 * side + 192, 128 * zc : 128 * zc + 128]

    partial(1 - core, gsend)
    send("g2core", gsend, grecv, sibling)
    partial(core, gown)
    load_basis.wait()

    def chunk(j):
        za, zb = place(-j), place(j + 1)
        if j == 0:
            gather_sibling("a", act_slot, 0)
        else:
            gather_sibling("a", act_slot, -j)
        gather_sibling("a", act_slot, j + 1)
        left = jnp.concatenate(
            [
                jnp.concatenate([acts[kk, pp, za].reshape(96, quarter), acts[kk, pp, zb].reshape(96, quarter)], axis=0)
                for kk in (0, 1)
                for pp in (0, 1)
            ],
            axis=1,
        )
        part[...] = jnp.dot(left, basis[...], preferred_element_type=F32).reshape(part.shape)
        for rel in (1, 2, 3):
            send_y[j, rel - 1] = part[ring(y + rel, NY)].astype(BF16)
            send(("s2", j, rel), send_y.at[j, rel - 1], recv_y.at[j, rel - 1], around[rel - 1])
        own_y[j] = part[y]

    def sum_y(j):
        total = own_y[j]
        for rel in (1, 2, 3):
            arrive(("s2", j, rel), recv_y.at[j, rel - 1])
            total = total + recv_y[j, rel - 1].astype(F32)
        half_x[j] = total.reshape(2, 24, -1)
        send(("s2x", j), half_x.at[j, 1 - xh], recv_x.at[j], across)

    def sum_x(j):
        arrive(("s2x", j), recv_x.at[j])
        done_x[j // 2, pl.ds(24 * (j % 2), 24)] = half_x[j, xh] + recv_x[j]

    def spread(p):
        rot_raw[p, y, xh] = done_x[p].astype(BF16)
        ref = rot_raw.at[p, y, xh]
        for rel in (1, 2, 3):
            send(("s3", p, rel, 0), ref, ref, around[rel - 1])
        send(("s3", p), ref, ref, across)

    def spread_on(p):
        ref = rot_raw.at[p, y, 1 - xh]
        arrive(("s3", p), ref)
        for rel in (1, 2, 3):
            send(("s3", p, rel, 1), ref, ref, around[rel - 1])

    def collect(p):
        for rel in (1, 2, 3):
            came = ring(y - rel, NY)
            arrive(("s3", p, rel, 0), rot_raw.at[p, came, xh])
            arrive(("s3", p, rel, 1), rot_raw.at[p, came, 1 - xh])
        whole = rot_raw[p].astype(F32)
        for odd in (0, 1):
            j = 2 * p + odd
            piece = whole[:, :, 24 * odd : 24 * odd + 24, :]
            rot[place(-j)] = piece[0:2].reshape(96, -1).astype(BF16)
            rot[place(j + 1)] = piece[2:4].reshape(96, -1).astype(BF16)

    def grad_beside():
        arrive("g2core", grecv)
        gx_send[...] = (gown[1 - xl] + grecv[1 - xl]).astype(BF16)
        send("g2x", gx_send, gx_recv, beside)

    def grad_sum():
        arrive("g2x", gx_recv)
        gsum[...] = gown[xl] + grecv[xl] + gx_recv[...].astype(F32)

    def length(way, part_no):
        return 4 if way == part_no else 3

    def grad_ring(step):
        for way in (0, 1):
            sign = 1 if way == 0 else -1
            for part_no in (0, 1):
                hops = length(way, part_no)
                if step > hops:
                    continue
                dest = place(sign * (hops - step + 1))
                value = gsum[dest, pl.ds(96 * part_no, 96)]
                if step > 1:
                    arrive(("g2", way, part_no, step - 1), ring_recv.at[way, part_no, step - 2])
                    value = value + ring_recv[way, part_no, step - 2]
                ring_send[way, part_no, step - 1] = value
                send(
                    ("g2", way, part_no, step),
                    ring_send.at[way, part_no, step - 1],
                    ring_recv.at[way, part_no, step - 1],
                    up[way],
                )

    def grad_end():
        for part_no in (0, 1):
            value = gsum[z, pl.ds(96 * part_no, 96)]
            for way in (0, 1):
                hops = length(way, part_no)
                arrive(("g2", way, part_no, hops), ring_recv.at[way, part_no, hops - 1])
                value = value + ring_recv[way, part_no, hops - 1]
            grot[2 * core + xl, z, pl.ds(96 * part_no, 96)] = value.astype(BF16)
        for part_no in (0, 1):
            gather_put("g", grad_slot, 0, part_no)

    gather_steps("a", act_slot, 1)
    grad_beside()
    chunk(0)
    gather_steps("a", act_slot, 2)
    sum_y(0)
    chunk(1)
    grad_sum()
    grad_ring(1)
    sum_x(0)
    gather_steps("a", act_slot, 3)
    sum_y(1)
    grad_ring(2)
    chunk(2)
    sum_x(1)
    spread(0)
    gather_steps("a", act_slot, 4)
    spread_on(0)
    sum_y(2)
    grad_ring(3)
    chunk(3)
    sum_x(2)
    grad_ring(4)
    sum_y(3)
    grad_end()
    sum_x(3)
    spread(1)
    for part_no in (0, 1):
        gather_beside("g", grad_slot, part_no)
    spread_on(1)
    collect(0)
    gather_steps("g", grad_slot, 1)
    gather_steps("g", grad_slot, 2)
    gather_steps("g", grad_slot, 3)
    gather_steps("g", grad_slot, 4)
    collect(1)
    out_act = pltpu.make_async_copy(rot, act_out, local_sem.at[0])
    out_act.start()
    for zoff in (0, 1, -1, 2, -2, 3, -3, 4):
        gather_sibling("g", grad_slot, zoff)
    out_grad = pltpu.make_async_copy(grot, grad_out, local_sem.at[1])
    out_grad.start()
    for one in sent:
        one.wait_send()
    out_act.wait()
    out_grad.wait()


def tiles(act_ref, grad_ref, out_ref):
    total = None
    for seq in range(2):
        left = act_ref[4 * seq : 4 * seq + 4].reshape(384, act_ref.shape[2])
        right = jnp.concatenate(
            [grad_ref[2 * seq : 2 * seq + 2, zc].reshape(384, 128) for zc in range(2)], axis=1
        )
        tile = lax.dot_general(left, right, (((0,), (0,)), ((), ())), preferred_element_type=F32)
        total = tile * tile if total is None else total + tile * tile
    out_ref[...] = total * F32(0.5)


def on_device(activations, out_grads, in_basis, out_basis):
    rows, depth = activations.shape
    wide = in_basis.shape[1]
    vmem = pl.BlockSpec(memory_space=pltpu.VMEM)
    hbm = pl.BlockSpec(memory_space=pl.ANY)
    act_rotated, grad_rotated = pl.pallas_call(
        exchange,
        out_shape=(
            jax.ShapeDtypeStruct((NZ, 96, wide), BF16),
            jax.ShapeDtypeStruct((4, NZ, 192, 128), BF16),
        ),
        in_specs=[vmem, vmem, hbm, hbm],
        out_specs=(hbm, hbm),
        scratch_shapes=[
            pltpu.VMEM(in_basis.shape, BF16),
            pltpu.VMEM(out_basis.shape, BF16),
            pltpu.VMEM((4, rows, depth // 2), F32),
            pltpu.VMEM((2, 2, NZ, 2, 48, depth // 4), BF16),
            pltpu.VMEM((4, 48, wide), F32),
            pltpu.VMEM((4, 3, 48, wide), BF16),
            pltpu.VMEM((4, 3, 48, wide), BF16),
            pltpu.VMEM((4, 48, wide), F32),
            pltpu.VMEM((4, 2, 24, wide), F32),
            pltpu.VMEM((4, 24, wide), F32),
            pltpu.VMEM((2, 48, wide), F32),
            pltpu.VMEM((2, NY, 2, 48, wide), BF16),
            pltpu.VMEM((NZ, 96, wide), BF16),
            pltpu.VMEM((8, 96, 256), BF16),
            pltpu.VMEM((2, NZ, 192, 128), F32),
            pltpu.VMEM((2, NZ, 192, 128), F32),
            pltpu.VMEM((2, NZ, 192, 128), F32),
            pltpu.VMEM((NZ, 192, 128), BF16),
            pltpu.VMEM((NZ, 192, 128), BF16),
            pltpu.VMEM((NZ, 192, 128), F32),
            pltpu.VMEM((2, 2, 4, 96, 128), F32),
            pltpu.VMEM((2, 2, 4, 96, 128), F32),
            pltpu.VMEM((4, NZ, 192, 128), BF16),
            pltpu.SemaphoreType.DMA((COPIES,)),
            pltpu.SemaphoreType.DMA((COPIES,)),
            pltpu.SemaphoreType.DMA((2,)),
        ],
        compiler_params=pltpu.CompilerParams(
            collective_id=0, has_side_effects=True, vmem_limit_bytes=VMEM_LIMIT
        ),
    )(activations, out_grads, in_basis, out_basis)
    return pl.pallas_call(
        tiles,
        grid=(4,),
        out_shape=jax.ShapeDtypeStruct((wide, 1024), F32),
        in_specs=[
            pl.BlockSpec((NZ, 96, wide), lambda i: (0, 0, 0)),
            pl.BlockSpec((4, 2, 192, 128), lambda i: (0, i, 0, 0)),
        ],
        out_specs=pl.BlockSpec((wide, 256), lambda i: (0, i)),
        compiler_params=pltpu.CompilerParams(vmem_limit_bytes=VMEM_LIMIT),
    )(act_rotated, grad_rotated)


def solution(mesh):
    placed = (P("row", "col"), P("col", "row"), P("col", "row"), P("row", "col"))
    return jax.shard_map(
        on_device, mesh=mesh, in_specs=placed, out_specs=P("row", "col"), check_vma=False
    )
```

time: 318 us -> 88.3 us (0.28)
  the two profiles are of different devices: /device:TPU:98 before, /device:TPU:1 now
where the time goes in v1:
time: 88.3 us; the launch traced here: 88.2 us
  Pallas kernels  88.2 us (100%)
    pallas_call x1, Pallas kernels, on_device(): pl.pallas_call(exchange, out_shape=(jax.ShapeDtypeStruct((NZ, 96, wide),...  82.3 us
    pallas_call x1, Pallas kernels, on_device(): pl.pallas_call(tiles, grid=(4,), out_shape=jax.ShapeDtypeStruct((wide, 10...  5.87 us

profile of v1, /device:TPU:1, one launch (start us, length us, event | category | flops | bytes accessed | tf_op | source)
XLA Modules:
  0.0 88.2 jit_solution(36693197763514569)
XLA Ops:
  0.0 82.3 %shard_map.46 = (bf16[8,96,896]{2,1,0:T(8,128)(2,1)}, bf16[4,8,192,128]{3,2,1,0:T(8,128)(2,1)}) custom-call(bf16[24,3584]{1,0:T(8,128)(2,1)} %act_ref.1, bf16[96,256]{1,0:T(8,128)(2,1)} %grad_ref.1, bf16[3584,896]{1,0:T(8,128)(2,1)} %in_basis.1, bf16[256,1024]{1,0:T(8,128)(2,1)} %out_basis.1), custom_call_target="tpu_custom_call" | custom-call | tf_op jit(solution)/shard_map/pallas_call | solution.py:321
  82.3 5.9 %shard_map.47 = f32[896,1024]{1,0:T(8,128)} custom-call(bf16[8,96,896]{2,1,0:T(8,128)(2,1)} %get-tuple-element.7.act_ref, bf16[4,8,192,128]{3,2,1,0:T(8,128)(2,1)} %get-tuple-element.8.grad_ref), custom_call_target="tpu_custom_call" | custom-call | tf_op jit(solution)/shard_map/pallas_call | solution.py:361

commit v2 on v0

v2 whole, which is shorter than its diff:
```python
import functools

import jax
import jax.numpy as jnp
from jax import lax
from jax.experimental import pallas as pl
from jax.experimental.pallas import tpu as pltpu
from jax.sharding import PartitionSpec as P

MESH = pl.DeviceIdType.MESH
F32 = jnp.float32
BF16 = jnp.bfloat16
NZ, NY = 8, 4
COPIES = 264
VMEM_LIMIT = 58 * 2**20
FAR = (4, 3, -3, 2, -2, 1, -1, 0)
CHUNKS = ((0,), (1, -1), (2, -2), (3, -3), (4,))
SLOT = (0, 0, 1, 2, 1)
DIRECT = (False, False, False, False, True)
ORDER = (
    "pair", "ga", "a0", "gb", "ax", "a10", "a11", "gp", "basis", "c0", "a20", "gx", "c1", "a21", "gs0", "r0", "a30", "gs1",
    "r1", "c2", "y0", "gs2", "r2", "a31", "t0", "y1", "ge", "a40", "gy", "a41", "c3", "h10", "t1", "c4", "h11", "y2",
    "h20", "t2", "h21", "y3", "h30", "y4", "h31", "t3", "h40", "h41", "t4", "u0", "u1", "u2", "u3", "u4", "gf",
)


def ring(value, size):
    return lax.rem(value + size, size)


def exchange(
    act_ref, grad_ref, in_basis, out_basis, act_out, grad_out,
    basis, obasis, pair, acts, part, send_y, recv_y, own_y, rot_raw,
    thin, thin_send, thin_recv, thin_own, thin_raw, rot,
    grads, gsend, grecv, gown, gx_send, gx_recv, gsum, ring_send, ring_recv, grot,
    send_sem, recv_sem, local_sem,
):
    row, col = lax.axis_index("row"), lax.axis_index("col")
    z, xl, core = row // 4, lax.rem(row // 2, 2), lax.rem(row, 2)
    y, xh = col // 2, lax.rem(col, 2)

    def at(z=z, xl=xl, core=core, y=y, xh=xh):
        return (z * 4 + xl * 2 + core, y * 2 + xh)

    sibling, beside, across = at(core=1 - core), at(xl=1 - xl), at(xh=1 - xh)
    up = (at(z=ring(z + 1, NZ)), at(z=ring(z - 1, NZ)))
    around = [at(y=ring(y + rel, NY)) for rel in (1, 2, 3)]
    members = [(rel, side) for rel in range(NY) for side in (0, 1)][1:]
    member = {(rel, side): at(y=ring(y + rel, NY), xh=1 - xh if side else xh) for rel, side in members}
    ids, sent, stored = {}, [], []

    def place(zoff):
        return ring(z + zoff, NZ)


    def copy(key, src, dst, device):
        number = ids.setdefault(key, len(ids))
        return pltpu.make_async_remote_copy(
            src_ref=src, dst_ref=dst, send_sem=send_sem.at[number], recv_sem=recv_sem.at[number],
            device_id=device, device_id_type=MESH,
        )

    def send(key, src, dst, device):
        one = copy(key, src, dst, device)
        one.start()
        sent.append(one)

    def arrive(key, dst):
        copy(key, dst, dst, sibling).wait_recv()

    load_basis = pltpu.make_async_copy(in_basis, basis, local_sem.at[8])
    load_obasis = pltpu.make_async_copy(out_basis, obasis, local_sem.at[9])
    load_obasis.start()
    load_basis.start()

    barrier = pltpu.get_barrier_semaphore()
    near = [sibling, beside, *(at(z=place(zoff)) for zoff in FAR[:-1]), *member.values()]
    for device in near:
        pl.semaphore_signal(barrier, inc=1, device_id=device, device_id_type=MESH)
    half = act_ref.shape[1] // 2
    quarter = half // 2
    mine = act_ref[...].astype(F32)
    for number in range(2):
        pair[2 + number] = mine[:, number * half : (number + 1) * half]
    pair[core] = pair[2 + core]
    grads[col] = grad_ref[...]
    pl.semaphore_wait(barrier, len(near))

    def act_slot(zz, q, part_no, side=0):
        kk = core if side == 0 else 1 - core
        return acts.at[kk, part_no, zz, xl if q == 0 else 1 - xl]

    def grad_slot(zz, q, part_no, side=0):
        kk = core if side == 0 else 1 - core
        return grot.at[2 * kk + (xl if q == 0 else 1 - xl), zz, pl.ds(96 * part_no, 96)]

    def gather_put(name, slot, q, part_no):
        ref = slot(z, q, part_no)
        for way in (0, 1):
            send((name, way, 1, q, part_no), ref, ref, up[way])
        if q == 0:
            send((name, "x", part_no), ref, ref, beside)
        send((name, "sib", 0, q, part_no), ref, ref, sibling)

    def gather_beside(name, slot, part_no):
        arrive((name, "x", part_no), slot(z, 1, part_no))
        gather_put(name, slot, 1, part_no)

    def gather_step(name, slot, step, way, q, part_no):
        if step == 4 and part_no != way:
            return
        zoff = 4 if step == 4 else (-step if way == 0 else step)
        ref = slot(place(zoff), q, part_no)
        arrive((name, way, step, q, part_no), ref)
        if step < 3 or (step == 3 and part_no == way):
            send((name, way, step + 1, q, part_no), ref, ref, up[way])
        send((name, "sib", zoff, q, part_no), ref, ref, sibling)

    def gather_steps(name, slot, step, q):
        for part_no in (0, 1):
            for way in (0, 1):
                gather_step(name, slot, step, way, q, part_no)

    def gather_sibling(name, slot, zoff):
        for q in (0, 1):
            for part_no in (0, 1):
                arrive((name, "sib", zoff, q, part_no), slot(place(zoff), q, part_no, 1))

    def partial(seq, ref):
        got = jnp.dot(grads[pl.ds(4 * seq, 4)].reshape(384, 256), obasis[...], preferred_element_type=F32)
        for side in range(2):
            for zc in range(NZ):
                ref[side, zc] = got[192 * side : 192 * side + 192, 128 * zc : 128 * zc + 128]

    def rotate(zoffs):
        for zoff in zoffs:
            gather_sibling("a", act_slot, zoff)
        left = jnp.concatenate(
            [
                jnp.concatenate([acts[kk, pp, place(zoff)].reshape(96, quarter) for zoff in zoffs], axis=0)
                for kk in (0, 1)
                for pp in (0, 1)
            ],
            axis=1,
        )
        return jnp.dot(left, basis[...], preferred_element_type=F32)

    def piece_of(wide, yy, hh):
        return (hh, yy) if wide else (2 * lax.rem(yy, 2) + hh, yy // 2)

    def chunk(j):
        zoffs, wide = CHUNKS[j], len(CHUNKS[j]) == 2
        got = rotate(zoffs)
        if wide:
            for n, at_col in enumerate((0, 384)):
                part[n] = got[:, at_col : at_col + 512].reshape(4, 48, 512)
        else:
            for n, at_col in enumerate((0, 256, 512, 640)):
                thin[n] = got[:, at_col : at_col + 256].reshape(2, 48, 256)
        parts, out, came, own = (part, send_y, recv_y, own_y) if wide else (thin, thin_send, thin_recv, thin_own)
        i = SLOT[j]
        for n, (rel, side) in enumerate(members):
            a, b = piece_of(wide, ring(y + rel, NY), 1 - xh if side else xh)
            out[i, n] = parts[a, b].astype(BF16)
            send(("s2", j, n), out.at[i, n], came.at[i, n], member[rel, side])
        a, b = piece_of(wide, y, xh)
        own[i] = parts[a, b]

    def sum_up(j):
        wide, i = len(CHUNKS[j]) == 2, SLOT[j]
        came, own, raw = (recv_y, own_y, rot_raw) if wide else (thin_recv, thin_own, thin_raw)
        total = own[i]
        for n in range(7):
            arrive(("s2", j, n), came.at[i, n])
            total = total + came[i, n].astype(F32)
        raw[i, y, xh] = total.astype(BF16)
        ref = raw.at[i, y, xh]
        if DIRECT[j]:
            for rel, side in members:
                send(("s3", j, rel, side), ref, ref, member[rel, side])
        else:
            send(("s3", j, 0, 1), ref, ref, across)
            for rel in (1, 2, 3):
                send(("s3", j, rel, 0), ref, ref, around[rel - 1])

    def spread_on(j):
        raw = rot_raw if len(CHUNKS[j]) == 2 else thin_raw
        ref = raw.at[SLOT[j], y, 1 - xh]
        arrive(("s3", j, 0, 1), ref)
        if not DIRECT[j]:
            for rel in (1, 2, 3):
                send(("s3", j, rel, 1), ref, ref, around[rel - 1])

    def collect(j):
        zoffs, i = CHUNKS[j], SLOT[j]
        wide = len(zoffs) == 2
        raw = rot_raw if wide else thin_raw
        for rel in (1, 2, 3):
            for side in (0, 1):
                arrive(("s3", j, rel, side), raw.at[i, ring(y - rel, NY), 1 - xh if side else xh])
        if wide:
            whole = jnp.concatenate([raw[i, :, 0], raw[i, :, 1][:, :, 128:]], axis=2)
        else:
            halves = [
                jnp.concatenate(
                    [raw[i, 2 * n, 0], raw[i, 2 * n, 1], raw[i, 2 * n + 1, 0], raw[i, 2 * n + 1, 1][:, 128:]], axis=1
                )
                for n in (0, 1)
            ]
        for n, zoff in enumerate(zoffs):
            zz = place(zoff)
            if wide:
                rot[zz] = whole[2 * n : 2 * n + 2].reshape(96, -1)
            else:
                rot[zz] = jnp.concatenate(halves, axis=0)
            one = pltpu.make_async_copy(rot.at[zz], act_out.at[zz], local_sem.at[zoff + 3])
            one.start()
            stored.append(one)

    def grad_beside():
        arrive(("g2core", 0), grecv.at[1 - xl])
        for zoff in FAR:
            zc = place(zoff)
            gx_send[zc] = (gown[1 - xl, zc] + grecv[1 - xl, zc]).astype(BF16)
            send(("g2x", zoff), gx_send.at[zc], gx_recv.at[zc], beside)
        arrive(("g2core", 1), grecv.at[xl])

    def grad_sum(offsets):
        for zoff in offsets:
            zc = place(zoff)
            arrive(("g2x", zoff), gx_recv.at[zc])
            gsum[zc] = gown[xl, zc] + grecv[xl, zc] + gx_recv[zc].astype(F32)

    def grad_spread(offsets):
        for zoff in offsets:
            n = zoff + 3
            ring_send[n] = gsum[place(zoff)].astype(BF16)
            send(("g2", zoff), ring_send.at[n], ring_recv.at[n], at(z=place(zoff)))

    def grad_end():
        value = gsum[z]
        for zoff in FAR[:-1]:
            arrive(("g2", zoff), ring_recv.at[zoff + 3])
            value = value + ring_recv[zoff + 3].astype(F32)
        grot[2 * core + xl, z] = value.astype(BF16)
        for part_no in (0, 1):
            gather_put("g", grad_slot, 0, part_no)

    def act_pair():
        send("pair", pair.at[3 - core], pair.at[core], sibling)

    def act_start():
        arrive("pair", pair.at[1 - core])
        block = pair[0:2].reshape(48, half).astype(BF16)
        for part_no in (0, 1):
            acts[core, part_no, z, xl] = block[:, part_no * quarter : (part_no + 1) * quarter]
        for part_no in (0, 1):
            gather_put("a", act_slot, 0, part_no)

    def act_beside():
        for part_no in (0, 1):
            gather_beside("a", act_slot, part_no)

    def grad_start():
        send(("g1", 0), grads.at[col], grads.at[col], across)
        for rel in (1, 2, 3):
            send(("g1", rel, 0), grads.at[col], grads.at[col], around[rel - 1])

    def grad_on():
        other = y * 2 + 1 - xh
        arrive(("g1", 0), grads.at[other])
        for rel in (1, 2, 3):
            send(("g1", rel, 1), grads.at[other], grads.at[other], around[rel - 1])

    def grad_partial():
        for rel in (1, 2, 3):
            came = ring(y - rel, NY) * 2
            arrive(("g1", rel, 0), grads.at[came + xh])
            arrive(("g1", rel, 1), grads.at[came + 1 - xh])
        load_obasis.wait()
        partial(1 - core, gsend)
        for n, side in enumerate((1 - xl, xl)):
            send(("g2core", n), gsend.at[side], grecv.at[side], sibling)
        partial(core, gown)

    def grad_gather_start():
        for part_no in (0, 1):
            gather_beside("g", grad_slot, part_no)

    out_grad = pltpu.make_async_copy(grot, grad_out, local_sem.at[10])

    def grad_finish():
        for zoff in (0, 1, -1, 2, -2, 3, -3, 4):
            gather_sibling("g", grad_slot, zoff)
        out_grad.start()

    def act_siblings():
        for zoff in (0, 1, -1, 2, -2, 3, -3, 4):
            gather_sibling("a", act_slot, zoff)

    steps = {
        "pair": act_pair, "ga": grad_start, "a0": act_start, "gb": grad_on, "ax": act_beside, "gp": grad_partial,
        "gx": grad_beside, "ge": grad_end, "gy": grad_gather_start, "gf": grad_finish,
        "basis": load_basis.wait, "ob": load_obasis.wait, "asib": act_siblings, "og": out_grad.start,
    }
    for n, offsets in enumerate((FAR[:3], FAR[3:5], FAR[5:])):
        steps[f"gs{n}"] = functools.partial(grad_sum, offsets)
    for n in range(4):
        for q in (0, 1):
            steps[f"a{n + 1}{q}"] = functools.partial(gather_steps, "a", act_slot, n + 1, q)
            steps[f"h{n + 1}{q}"] = functools.partial(gather_steps, "g", grad_slot, n + 1, q)
    for n, offsets in enumerate((FAR[:3], FAR[3:5], FAR[5:7])):
        steps[f"r{n}"] = functools.partial(grad_spread, offsets)
    for n in range(5):
        steps[f"c{n}"] = functools.partial(chunk, n)
        steps[f"y{n}"] = functools.partial(sum_up, n)
        steps[f"t{n}"] = functools.partial(spread_on, n)
        steps[f"u{n}"] = functools.partial(collect, n)
    for name in ORDER:
        steps[name]()
    for one in sent:
        one.wait_send()
    for one in stored:
        one.wait()
    out_grad.wait()


def tiles(act_hbm, grad_hbm, out_hbm, act, grad, turned, out, in_sem, out_sem):
    wide = act.shape[2]
    loads = []
    for seq in range(2):
        for n, (src, dst, step) in enumerate(((act_hbm, act, 4), (grad_hbm, grad, 2))):
            rows = pl.ds(step * seq, step)
            loads.append(pltpu.make_async_copy(src.at[rows], dst.at[rows], in_sem.at[2 * seq + n]))
    for one in loads:
        one.start()
    stores = []
    for seq in range(2):
        loads[2 * seq].wait()
        turned[seq] = act[4 * seq : 4 * seq + 4].reshape(384, wide).T
        loads[2 * seq + 1].wait()
    for n in range(4):
        total = None
        for seq in range(2):
            right = jnp.concatenate(
                [grad[2 * seq : 2 * seq + 2, 2 * n + zc].reshape(384, 128) for zc in range(2)], axis=1
            )
            tile = jnp.dot(turned[seq], right, preferred_element_type=F32)
            total = tile * tile if total is None else total + tile * tile
        out[n] = total * F32(0.5)
        one = pltpu.make_async_copy(out.at[n], out_hbm.at[:, pl.ds(256 * n, 256)], out_sem.at[n])
        one.start()
        stores.append(one)
    for one in stores:
        one.wait()


def on_device(activations, out_grads, in_basis, out_basis):
    rows, depth = activations.shape
    wide = in_basis.shape[1]
    vmem = pl.BlockSpec(memory_space=pltpu.VMEM)
    hbm = pl.BlockSpec(memory_space=pl.ANY)
    act_rotated, grad_rotated = pl.pallas_call(
        exchange,
        out_shape=(
            jax.ShapeDtypeStruct((NZ, 96, wide), BF16),
            jax.ShapeDtypeStruct((4, NZ, 192, 128), BF16),
        ),
        in_specs=[vmem, vmem, hbm, hbm],
        out_specs=(hbm, hbm),
        scratch_shapes=[
            pltpu.VMEM(in_basis.shape, BF16),
            pltpu.VMEM(out_basis.shape, BF16),
            pltpu.VMEM((4, rows, depth // 2), F32),
            pltpu.VMEM((2, 2, NZ, 2, 48, depth // 4), BF16),
            pltpu.VMEM((2, NY, 48, 512), F32),
            pltpu.VMEM((3, 7, 48, 512), BF16),
            pltpu.VMEM((3, 7, 48, 512), BF16),
            pltpu.VMEM((3, 48, 512), F32),
            pltpu.VMEM((3, NY, 2, 48, 512), BF16),
            pltpu.VMEM((4, 2, 48, 256), F32),
            pltpu.VMEM((2, 7, 48, 256), BF16),
            pltpu.VMEM((2, 7, 48, 256), BF16),
            pltpu.VMEM((2, 48, 256), F32),
            pltpu.VMEM((2, NY, 2, 48, 256), BF16),
            pltpu.VMEM((NZ, 96, wide), BF16),
            pltpu.VMEM((8, 96, 256), BF16),
            pltpu.VMEM((2, NZ, 192, 128), F32),
            pltpu.VMEM((2, NZ, 192, 128), F32),
            pltpu.VMEM((2, NZ, 192, 128), F32),
            pltpu.VMEM((NZ, 192, 128), BF16),
            pltpu.VMEM((NZ, 192, 128), BF16),
            pltpu.VMEM((NZ, 192, 128), F32),
            pltpu.VMEM((NZ, 192, 128), BF16),
            pltpu.VMEM((NZ, 192, 128), BF16),
            pltpu.VMEM((4, NZ, 192, 128), BF16),
            pltpu.SemaphoreType.DMA((COPIES,)),
            pltpu.SemaphoreType.DMA((COPIES,)),
            pltpu.SemaphoreType.DMA((11,)),
        ],
        compiler_params=pltpu.CompilerParams(
            collective_id=0, has_side_effects=True, vmem_limit_bytes=VMEM_LIMIT
        ),
    )(activations, out_grads, in_basis, out_basis)
    return pl.pallas_call(
        tiles,
        out_shape=jax.ShapeDtypeStruct((wide, 1024), F32),
        in_specs=[hbm, hbm],
        out_specs=hbm,
        scratch_shapes=[
            pltpu.VMEM((NZ, 96, wide), BF16),
            pltpu.VMEM((4, NZ, 192, 128), BF16),
            pltpu.VMEM((2, wide, 384), BF16),
            pltpu.VMEM((4, wide, 256), F32),
            pltpu.SemaphoreType.DMA((4,)),
            pltpu.SemaphoreType.DMA((4,)),
        ],
        compiler_params=pltpu.CompilerParams(vmem_limit_bytes=VMEM_LIMIT),
    )(act_rotated, grad_rotated)


def solution(mesh):
    placed = (P("row", "col"), P("col", "row"), P("col", "row"), P("row", "col"))
    return jax.shard_map(
        on_device, mesh=mesh, in_specs=placed, out_specs=P("row", "col"), check_vma=False
    )
```

time: 318 us -> 83.2 us (0.26)
  the two profiles are of different devices: /device:TPU:98 before, /device:TPU:1 now
where the time goes in v2:
time: 83.2 us; the launch traced here: 83 us
  Pallas kernels  83 us (100%)
    pallas_call x1, Pallas kernels, on_device(): pl.pallas_call(exchange, out_shape=(jax.ShapeDtypeStruct((NZ, 96, wide),...  78.2 us
    pallas_call x1, Pallas kernels, on_device(): pl.pallas_call(tiles, out_shape=jax.ShapeDtypeStruct((wide, 1024), F32),...  4.85 us

profile of v2, /device:TPU:1, one launch (start us, length us, event | category | flops | bytes accessed | tf_op | source)
XLA Modules:
  0.0 83.0 jit_solution(14569425589787449436)
XLA Ops:
  0.0 78.2 %shard_map.46 = (bf16[8,96,896]{2,1,0:T(8,128)(2,1)}, bf16[4,8,192,128]{3,2,1,0:T(8,128)(2,1)}) custom-call(bf16[24,3584]{1,0:T(8,128)(2,1)} %act_ref.1, bf16[96,256]{1,0:T(8,128)(2,1)} %grad_ref.1, bf16[3584,896]{1,0:T(8,128)(2,1)} %in_basis.1, bf16[256,1024]{1,0:T(8,128)(2,1)} %out_basis.1), custom_call_target="tpu_custom_call" | custom-call | tf_op jit(solution)/shard_map/pallas_call | solution.py:363
  78.2 4.8 %shard_map.47 = f32[896,1024]{1,0:T(8,128)} custom-call(bf16[8,96,896]{2,1,0:T(8,128)(2,1)} %get-tuple-element.7.act_hbm, bf16[4,8,192,128]{3,2,1,0:T(8,128)(2,1)} %get-tuple-element.8.grad_hbm), custom_call_target="tpu_custom_call" | custom-call | tf_op jit(solution)/shard_map/pallas_call | solution.py:405

commit v3 on v2

--- a/solution.py
+++ b/solution.py
@@ -16,11 +16,14 @@
 FAR = (4, 3, -3, 2, -2, 1, -1, 0)
 CHUNKS = ((0,), (1, -1), (2, -2), (3, -3), (4,))
 SLOT = (0, 0, 1, 2, 1)
+FIRST = {"a": (1,), "g": (1, 2)}
+ONWARD = {"a": {1: (2,), 2: (3,), 3: (4,)}, "g": {2: (3, 4)}}
 DIRECT = (False, False, False, False, True)
 ORDER = (
-    "pair", "ga", "a0", "gb", "ax", "a10", "a11", "gp", "basis", "c0", "a20", "gx", "c1", "a21", "gs0", "r0", "a30", "gs1",
-    "r1", "c2", "y0", "gs2", "r2", "a31", "t0", "y1", "ge", "a40", "gy", "a41", "c3", "h10", "t1", "c4", "h11", "y2",
-    "h20", "t2", "h21", "y3", "h30", "y4", "h31", "t3", "h40", "h41", "t4", "u0", "u1", "u2", "u3", "u4", "gf",
+    "pair", "ga", "a0", "gb", "ax", "a10", "a11", "gp", "basis", "c0", "a20", "gx", "c1", "a21", "y0", "gs0", "r0", "a30",
+    "gs1", "r1", "c2", "t0", "gs2", "r2", "a31", "c3", "y1", "a40", "a41", "c4", "f0", "ge", "gy", "t1", "y2", "h20",
+    "f1", "h21", "t2", "h10", "h11", "y3", "h30", "f2", "y4", "h31", "t3", "k0", "u0", "k1", "u1", "h40", "h41", "t4",
+    "f3", "k2", "u2", "k3", "u3", "u4", "k4",
 )
 
 
@@ -43,7 +46,6 @@
         return (z * 4 + xl * 2 + core, y * 2 + xh)
 
     sibling, beside, across = at(core=1 - core), at(xl=1 - xl), at(xh=1 - xh)
-    up = (at(z=ring(z + 1, NZ)), at(z=ring(z - 1, NZ)))
     around = [at(y=ring(y + rel, NY)) for rel in (1, 2, 3)]
     members = [(rel, side) for rel in range(NY) for side in (0, 1)][1:]
     member = {(rel, side): at(y=ring(y + rel, NY), xh=1 - xh if side else xh) for rel, side in members}
@@ -94,10 +96,14 @@
         kk = core if side == 0 else 1 - core
         return grot.at[2 * kk + (xl if q == 0 else 1 - xl), zz, pl.ds(96 * part_no, 96)]
 
+    def along(way, hops):
+        return at(z=place(hops if way == 0 else -hops))
+
     def gather_put(name, slot, q, part_no):
         ref = slot(z, q, part_no)
         for way in (0, 1):
-            send((name, way, 1, q, part_no), ref, ref, up[way])
+            for step in FIRST[name]:
+                send((name, way, step, q, part_no), ref, ref, along(way, step))
         if q == 0:
             send((name, "x", part_no), ref, ref, beside)
         send((name, "sib", 0, q, part_no), ref, ref, sibling)
@@ -112,8 +118,9 @@
         zoff = 4 if step == 4 else (-step if way == 0 else step)
         ref = slot(place(zoff), q, part_no)
         arrive((name, way, step, q, part_no), ref)
-        if step < 3 or (step == 3 and part_no == way):
-            send((name, way, step + 1, q, part_no), ref, ref, up[way])
+        for later in ONWARD[name].get(step, ()):
+            if later < 4 or part_no == way:
+                send((name, way, later, q, part_no), ref, ref, along(way, later - step))
         send((name, "sib", zoff, q, part_no), ref, ref, sibling)
 
     def gather_steps(name, slot, step, q):
@@ -287,21 +294,22 @@
         for part_no in (0, 1):
             gather_beside("g", grad_slot, part_no)
 
-    out_grad = pltpu.make_async_copy(grot, grad_out, local_sem.at[10])
-
-    def grad_finish():
-        for zoff in (0, 1, -1, 2, -2, 3, -3, 4):
+    def grad_store(offsets):
+        for zoff in offsets:
             gather_sibling("g", grad_slot, zoff)
-        out_grad.start()
-
-    def act_siblings():
-        for zoff in (0, 1, -1, 2, -2, 3, -3, 4):
-            gather_sibling("a", act_slot, zoff)
+            zz = place(zoff)
+            one = pltpu.make_async_copy(grot.at[:, zz], grad_out.at[:, zz], local_sem.at[zoff + 13])
+            one.start()
+            stored.append(one)
+
+    def flush():
+        while len(sent) > 48:
+            sent.pop(0).wait_send()
 
     steps = {
         "pair": act_pair, "ga": grad_start, "a0": act_start, "gb": grad_on, "ax": act_beside, "gp": grad_partial,
-        "gx": grad_beside, "ge": grad_end, "gy": grad_gather_start, "gf": grad_finish,
-        "basis": load_basis.wait, "ob": load_obasis.wait, "asib": act_siblings, "og": out_grad.start,
+        "gx": grad_beside, "ge": grad_end, "gy": grad_gather_start,
+        "basis": load_basis.wait, "f0": flush, "f1": flush, "f2": flush, "f3": flush,
     }
     for n, offsets in enumerate((FAR[:3], FAR[3:5], FAR[5:])):
         steps[f"gs{n}"] = functools.partial(grad_sum, offsets)
@@ -309,6 +317,8 @@
         for q in (0, 1):
             steps[f"a{n + 1}{q}"] = functools.partial(gather_steps, "a", act_slot, n + 1, q)
             steps[f"h{n + 1}{q}"] = functools.partial(gather_steps, "g", grad_slot, n + 1, q)
+    for n, offsets in enumerate(((0,), (1, -1), (2, -2), (3, -3), (4,))):
+        steps[f"k{n}"] = functools.partial(grad_store, offsets)
     for n, offsets in enumerate((FAR[:3], FAR[3:5], FAR[5:7])):
         steps[f"r{n}"] = functools.partial(grad_spread, offsets)
     for n in range(5):
@@ -322,7 +332,6 @@
         one.wait_send()
     for one in stored:
         one.wait()
-    out_grad.wait()
 
 
 def tiles(act_hbm, grad_hbm, out_hbm, act, grad, turned, out, in_sem, out_sem):
@@ -396,7 +405,7 @@
             pltpu.VMEM((4, NZ, 192, 128), BF16),
             pltpu.SemaphoreType.DMA((COPIES,)),
             pltpu.SemaphoreType.DMA((COPIES,)),
-            pltpu.SemaphoreType.DMA((11,)),
+            pltpu.SemaphoreType.DMA((18,)),
         ],
         compiler_params=pltpu.CompilerParams(
             collective_id=0, has_side_effects=True, vmem_limit_bytes=VMEM_LIMIT

time: 83.2 us -> 82 us (0.986)
  Pallas kernels: 83 us -> 81.8 us
    pallas_call x1, Pallas kernels: 78.2 us -> 77 us  [on_device(): pl.pallas_call(exchange, out_shape=(jax.ShapeDtypeStruct((NZ, 96, wide),...]
where the time goes in v3:
time: 82 us; the launch traced here: 81.8 us
  Pallas kernels  81.8 us (100%)
    pallas_call x1, Pallas kernels, on_device(): pl.pallas_call(exchange, out_shape=(jax.ShapeDtypeStruct((NZ, 96, wide),...  77 us
    pallas_call x1, Pallas kernels, on_device(): pl.pallas_call(tiles, out_shape=jax.ShapeDtypeStruct((wide, 1024), F32),...  4.85 us

profile of v3, /device:TPU:1, one launch (start us, length us, event | category | flops | bytes accessed | tf_op | source)
XLA Modules:
  0.0 81.8 jit_solution(11930502538062107481)
XLA Ops:
  0.0 77.0 %shard_map.46 = (bf16[8,96,896]{2,1,0:T(8,128)(2,1)}, bf16[4,8,192,128]{3,2,1,0:T(8,128)(2,1)}) custom-call(bf16[24,3584]{1,0:T(8,128)(2,1)} %act_ref.1, bf16[96,256]{1,0:T(8,128)(2,1)} %grad_ref.1, bf16[3584,896]{1,0:T(8,128)(2,1)} %in_basis.1, bf16[256,1024]{1,0:T(8,128)(2,1)} %out_basis.1), custom_call_target="tpu_custom_call" | custom-call | tf_op jit(solution)/shard_map/pallas_call | solution.py:372
  77.0 4.8 %shard_map.47 = f32[896,1024]{1,0:T(8,128)} custom-call(bf16[8,96,896]{2,1,0:T(8,128)(2,1)} %get-tuple-element.7.act_hbm, bf16[4,8,192,128]{3,2,1,0:T(8,128)(2,1)} %get-tuple-element.8.grad_hbm), custom_call_target="tpu_custom_call" | custom-call | tf_op jit(solution)/shard_map/pallas_call | solution.py:414

commit v4 on v3

--- a/solution.py
+++ b/solution.py
@@ -72,6 +72,8 @@
 
     load_basis = pltpu.make_async_copy(in_basis, basis, local_sem.at[8])
     load_obasis = pltpu.make_async_copy(out_basis, obasis, local_sem.at[9])
+    load_grads = pltpu.make_async_copy(grad_ref, grads.at[col], local_sem.at[18])
+    load_grads.start()
     load_obasis.start()
     load_basis.start()
 
@@ -85,7 +87,7 @@
     for number in range(2):
         pair[2 + number] = mine[:, number * half : (number + 1) * half]
     pair[core] = pair[2 + core]
-    grads[col] = grad_ref[...]
+    load_grads.wait()
     pl.semaphore_wait(barrier, len(near))
 
     def act_slot(zz, q, part_no, side=0):
@@ -375,7 +377,7 @@
             jax.ShapeDtypeStruct((NZ, 96, wide), BF16),
             jax.ShapeDtypeStruct((4, NZ, 192, 128), BF16),
         ),
-        in_specs=[vmem, vmem, hbm, hbm],
+        in_specs=[vmem, hbm, hbm, hbm],
         out_specs=(hbm, hbm),
         scratch_shapes=[
             pltpu.VMEM(in_basis.shape, BF16),
@@ -405,7 +407,7 @@
             pltpu.VMEM((4, NZ, 192, 128), BF16),
             pltpu.SemaphoreType.DMA((COPIES,)),
             pltpu.SemaphoreType.DMA((COPIES,)),
-            pltpu.SemaphoreType.DMA((18,)),
+            pltpu.SemaphoreType.DMA((19,)),
         ],
         compiler_params=pltpu.CompilerParams(
             collective_id=0, has_side_effects=True, vmem_limit_bytes=VMEM_LIMIT

time: 82 us -> 82 us (level)
  no operation moved by 1% of the time
where the time goes in v4:
time: 82 us; the launch traced here: 81.9 us
  Pallas kernels  81.8 us (100%)
    pallas_call x1, Pallas kernels, on_device(): pl.pallas_call(exchange, out_shape=(jax.ShapeDtypeStruct((NZ, 96, wide),...  77 us
    pallas_call x1, Pallas kernels, on_device(): pl.pallas_call(tiles, out_shape=jax.ShapeDtypeStruct((wide, 1024), F32),...  4.85 us

profile of v4, /device:TPU:1, one launch (start us, length us, event | category | flops | bytes accessed | tf_op | source)
XLA Modules:
  0.0 81.9 jit_solution(6684771934315163364)
XLA Ops:
  0.0 77.0 %shard_map.46 = (bf16[8,96,896]{2,1,0:T(8,128)(2,1)}, bf16[4,8,192,128]{3,2,1,0:T(8,128)(2,1)}) custom-call(bf16[24,3584]{1,0:T(8,128)(2,1)} %act_ref.1, bf16[96,256]{1,0:T(8,128)(2,1)} %grad_ref.1, bf16[3584,896]{1,0:T(8,128)(2,1)} %in_basis.1, bf16[256,1024]{1,0:T(8,128)(2,1)} %out_basis.1), custom_call_target="tpu_custom_call" | custom-call | tf_op jit(solution)/shard_map/pallas_call | solution.py:374
  77.0 4.8 %shard_map.47 = f32[896,1024]{1,0:T(8,128)} custom-call(bf16[8,96,896]{2,1,0:T(8,128)(2,1)} %get-tuple-element.7.act_hbm, bf16[4,8,192,128]{3,2,1,0:T(8,128)(2,1)} %get-tuple-element.8.grad_hbm), custom_call_target="tpu_custom_call" | custom-call | tf_op jit(solution)/shard_map/pallas_call | solution.py:416
